TPU v7x, 32 devices: a whole 2x2x4 slice. The times are simulated.
32 devices in a mesh: cell: 8 (over z, y), own: 4 (over x, core).
Axes of the slice: x: 2, y: 2, z: 4, core: 2. Of those that a mesh axis runs over, the one named last changes fastest.
Arguments:
- hist: bfloat16 [65536, 3, 256], P(('cell', 'own')), as said below
- dest: int32 [65536, 1], P(('cell', 'own')), may hold values from 0 to 31; in each aligned block of 2048 rows (0 to 2047, 2048 to 4095, ...) at most 128 rows name the same one
- cell_in: int32 [65536], P(('cell', 'own')), may hold values from 0 to 1023
- offsets: int32 [4, 32768], P(None, ('cell', 'own')), may hold values from -4 to 4
Outputs:
- multipliers: float32 [2, 6, 32768], P(None, None, ('cell', 'own'))
- fit_stat: float32 [2, 32768], P(None, ('cell', 'own'))
Inputs may be any that keep to these rules, and one draw needn't show every extreme that they name: `dest`: the rows of one device name each cell block at most 128 times, and in every draw some device names some block exactly 128 times. `hist`: Positive, every entry at least three ten-thousandths of its row's largest.
All inputs are finite; a program needn't handle non-finite values.
Results may differ from a plain program's by a relative error of at most 0.0022.
Values may be sent and summed in bfloat16 or wider, within the bound.
A program may use at most 64 MiB of HBM per device.

v0:
```python
import functools
import jax
import jax.numpy as jnp
import numpy as np
from jax import lax
from jax.experimental import pallas as pl
from jax.experimental.pallas import tpu as pltpu
from jax.sharding import PartitionSpec as P

SPEC = 2
MOM = 6
NEWTON = 8
NEIGH = 4
W = 4
TILE = 256
RIM = 8
BF = jnp.bfloat16
F32 = jnp.float32


def legendre_rows(levels, count):
    xpos = (2.0 * np.arange(levels) + 1.0) / levels - 1.0
    table = [np.ones_like(xpos), xpos]
    for order in range(1, count - 1):
        table.append(((2 * order + 1) * xpos * table[order] - order * table[order - 1]) / (order + 1))
    return np.stack(table, axis=0)


def product_weights(count):
    weights = {}
    for m in range(1, count + 1):
        for n in range(1, m + 1):
            series = np.polynomial.legendre.legmul(np.eye(m + 1)[m], np.eye(n + 1)[n])
            weights[m, n] = [(k, float(v)) for k, v in enumerate(series) if abs(v) > 1e-12]
    return weights


def halves(value):
    high = value.astype(BF)
    return high, (value - high.astype(F32)).astype(BF)


def fit_tables(levels):
    rows = np.zeros((16, levels))
    rows[: 2 * MOM + 1] = legendre_rows(levels, 2 * MOM + 1)
    high = np.asarray(rows, jnp.bfloat16)
    low = np.asarray(rows - high.astype(np.float64), jnp.bfloat16)
    gather = np.zeros((32, 2 * levels), jnp.bfloat16)
    gather[:16, :levels] = high
    gather[:16, levels:] = high
    gather[16:, :levels] = low
    spread = np.zeros((levels, 32), jnp.bfloat16)
    spread[:, 0:MOM] = high[1 : MOM + 1].T
    spread[:, 8 : 8 + MOM] = low[1 : MOM + 1].T
    spread[:, 16 : 16 + MOM] = high[1 : MOM + 1].T
    return jnp.asarray(gather), jnp.asarray(spread)


def fit_kernel(cell_ref, low_ref, high_ref, off_ref, gather_ref, spread_ref, lam_ref, stat_ref,
               ext, target, sums, lam, mu):
    cells = cell_ref.shape[0]
    levels = gather_ref.shape[1] // 2
    tiles = cells // TILE
    span = TILE + 2 * RIM
    ext[0:RIM, :] = low_ref[...]
    ext[RIM : RIM + cells, :] = cell_ref[...]
    ext[RIM + cells :, :] = high_ref[...]
    tn = (((0,), (0,)), ((), ()))

    def moments(value):
        high, low = halves(value)
        both = jnp.dot(gather_ref[...], jnp.concatenate([high, low], axis=0), preferred_element_type=F32)
        return both[:16] + both[16:]

    def exponent(group):
        value = lam[:, group, :]
        high = value.astype(BF).astype(F32)
        stacked = jnp.concatenate([high, high, value - high, jnp.zeros_like(high)], axis=0)
        return jnp.dot(spread_ref[...], stacked.astype(BF), preferred_element_type=F32)

    place = lax.broadcasted_iota(jnp.int32, (span, TILE), 0) - lax.broadcasted_iota(jnp.int32, (span, TILE), 1) - RIM
    level = lax.broadcasted_iota(jnp.int32, (levels, TILE), 0)
    for block in range(tiles):
        cols = slice(block * TILE, (block + 1) * TILE)
        picker = (place == 0).astype(F32)
        for j in range(NEIGH):
            picker = picker + (place == off_ref[j : j + 1, cols]).astype(F32)
        picker = picker.astype(BF)
        high, low = halves(ext[block * TILE : block * TILE + span, :])
        summed = lax.dot_general(high, picker, tn, preferred_element_type=F32) + lax.dot_general(
            low, picker, tn, preferred_element_type=F32
        )
        for s in range(SPEC):
            field = summed[s * levels : (s + 1) * levels]
            below = jnp.where(level == 0, 0.0, pltpu.roll(field, 1, 0))
            above = jnp.where(level == levels - 1, 0.0, pltpu.roll(field, levels - 1, 0))
            smooth = 1.0 + (0.5 * field + 0.25 * (below + above))
            group = s * tiles + block
            target[group] = smooth
            sums[:, group, :] = moments(smooth)
    inverse = 1.0 / sums[0]
    for m in range(MOM):
        mu[m] = sums[m + 1] * inverse
    lam[...] = jnp.zeros_like(lam)
    weights = product_weights(MOM)

    def step(_, carry):
        for group in range(SPEC * tiles):
            sums[:, group, :] = moments(jnp.exp(exponent(group)))
        inverse = 1.0 / sums[0]
        mean = [None] + [sums[k] * inverse for k in range(1, 2 * MOM + 1)]
        raw = [[None] * MOM for _ in range(MOM)]
        unit = [[None] * MOM for _ in range(MOM)]
        scale = [None] * MOM
        for row in range(MOM):
            for col in range(row + 1):
                total = -mean[row + 1] * mean[col + 1]
                if row == col:
                    total = total + 0.01
                for k, v in weights[row + 1, col + 1]:
                    total = total + (v if k == 0 else v * mean[k])
                for inner in range(col):
                    total = total - raw[row][inner] * unit[col][inner]
                if row == col:
                    scale[row] = 1.0 / total
                else:
                    raw[row][col] = total
                    unit[row][col] = total * scale[col]
        forward = []
        for row in range(MOM):
            total = mean[row + 1] - mu[row]
            for inner in range(row):
                total = total - unit[row][inner] * forward[inner]
            forward.append(total)
        backward = [None] * MOM
        for row in reversed(range(MOM)):
            total = forward[row] * scale[row]
            for inner in range(row + 1, MOM):
                total = total - unit[inner][row] * backward[inner]
            backward[row] = total
            lam[row] = lam[row] - 0.5 * total
        return carry

    lax.fori_loop(0, NEWTON, step, 0)
    for s in range(SPEC):
        for block in range(tiles):
            cols = slice(block * TILE, (block + 1) * TILE)
            group = s * tiles + block
            lam_ref[s, :, cols] = lam[0:MOM, group, :]
            value = exponent(group)
            norm = jnp.log(jnp.sum(jnp.exp(value), axis=0, keepdims=True))
            field = target[group]
            total = jnp.log(jnp.sum(field, axis=0, keepdims=True))
            ratio = (jnp.log(field) - value) + (norm - total)
            stat_ref[s : s + 1, cols] = (2.0 / levels) * jnp.sum(field * ratio, axis=0, keepdims=True)


def fit(cellhist, low, high, offsets):
    cells, width = cellhist.shape
    levels = width // SPEC
    groups = SPEC * cells // TILE
    gather, spread = fit_tables(levels)
    return pl.pallas_call(
        fit_kernel,
        out_shape=(
            jax.ShapeDtypeStruct((SPEC, MOM, cells), F32),
            jax.ShapeDtypeStruct((SPEC, cells), F32),
        ),
        in_specs=[pl.BlockSpec(memory_space=pltpu.VMEM)] * 6,
        out_specs=(pl.BlockSpec(memory_space=pltpu.VMEM),) * 2,
        scratch_shapes=[
            pltpu.VMEM((cells + 2 * RIM, width), F32),
            pltpu.VMEM((groups, levels, TILE), F32),
            pltpu.VMEM((16, groups, TILE), F32),
            pltpu.VMEM((8, groups, TILE), F32),
            pltpu.VMEM((8, groups, TILE), F32),
        ],
        compiler_params=pltpu.CompilerParams(vmem_limit_bytes=32 * 1024 * 1024),
        name="fit",
    )(cellhist, low, high, offsets, gather, spread)


def body(hist, dest, cell_in, offsets):
    rows = hist.shape[0]
    width = hist.shape[2]
    cells = offsets.shape[1]
    devices = lax.axis_size(("cell", "own"))
    capacity = 2 * rows // devices
    packed = jnp.sum(hist, axis=1, dtype=jnp.float32).astype(jnp.bfloat16)
    target_block = dest[:, 0]
    member = (target_block[:, None] == jnp.arange(devices, dtype=jnp.int32)[None, :]).astype(jnp.int32)
    ranks = jnp.sum((jnp.cumsum(member, axis=0) - 1) * member, axis=1)
    position = target_block * capacity + ranks
    send_rows = jnp.zeros((devices * capacity, width), jnp.bfloat16).at[position].set(packed)
    send_cells = jnp.full((devices * capacity,), -1, jnp.int32).at[position].set(cell_in)
    got_rows = lax.all_to_all(send_rows.reshape(devices, capacity, width), ("cell", "own"), split_axis=0, concat_axis=0, tiled=True)
    got_cells = lax.all_to_all(send_cells.reshape(devices, capacity), ("cell", "own"), split_axis=0, concat_axis=0, tiled=True)
    recv_rows = got_rows.reshape(devices * capacity, width)
    recv_cells = got_cells.reshape(devices * capacity)
    select = (recv_cells[None, :] == jnp.arange(cells, dtype=jnp.int32)[:, None]).astype(jnp.bfloat16)
    cellhist = jnp.dot(select, recv_rows, preferred_element_type=jnp.float32)
    forward = [(i, i + 1) for i in range(devices - 1)]
    backward = [(i + 1, i) for i in range(devices - 1)]
    low = lax.ppermute(cellhist[-RIM:], ("cell", "own"), forward)
    high = lax.ppermute(cellhist[:RIM], ("cell", "own"), backward)
    return fit(cellhist, low, high, offsets)


def solution(mesh):
    placed = (
        P(("cell", "own"), None, None),
        P(("cell", "own"), None),
        P(("cell", "own")),
        P(None, ("cell", "own")),
    )
    return jax.shard_map(
        body,
        mesh=mesh,
        in_specs=placed,
        out_specs=(P(None, None, ("cell", "own")), P(None, ("cell", "own"))),
        check_vma=False,
    )
```

profile of v0, /device:TPU:7, one launch (start us, length us, event | category | flops | bytes accessed | tf_op | source)
XLA Modules:
  0.0 115.9 jit_solution(7338658838440910765)
XLA Ops:
  0.6 0.0 copy-start.3
  0.6 0.8 fusion.6
  1.4 9.1 %reduce-window.6 = s32[32,16,128]{2,1,0:T(8,128)S(1)} reduce-window(s32[32,16,128]{2,1,0:T(8,128)S(1)} %fusion.6, s32[]{:T(128)} %constant.9.clone.1), window={size=1x1x128 pad=0_0x0_0x127_0}, to_apply=%region_0.0 | reduce-window | flops 8323072 | bytes 524292 | tf_op jit(solution)/shard_map/reduce-window
  10.5 0.1 slice.16
  10.6 0.2 copy.12
  10.9 0.2 reduce-window.9
  11.1 0.1 add_add_fusion
  11.2 0.0 copy-done.3
  11.2 0.1 fusion.5
  11.4 8.8 %scatter_custom_fusion = s32[4096]{0:T(1024)} fusion(s32[2048]{0:T(1024)S(1)} %bitcast.34, s32[2048]{0:T(1024)} %param.8, s32[]{:T(128)} %constant.7.clone.1), kind=kCustom, calls=%fused_computation.15 | custom fusion | bytes 16896 | tf_op jit(solution)/shard_map/scatter | solution.py:195
  20.2 6.4 %all-to-all-start = ((s32[32,1,128]{2,1,0:T(1,128)}), s32[32,1,128]{2,1,0:T(1,128)S(1)}, u32[]{:S(2)}, u32[]{:S(2)}) async-start(s32[32,1,128]{2,1,0:T(1,128)} %bitcast.7), calls=%async_computation | async-start | bytes 32768 | tf_op jit(solution)/shard_map/all_to_all | solution.py:197
  26.5 3.0 %reduce_sum.25 = bf16[2048,256]{1,0:T(8,128)(2,1)S(1)} reduce(bf16[2048,3,256]{2,0,1:T(8,128)(2,1)} %param.6, bf16[]{:T(256)} %constant.22.clone.1), dimensions={1}, to_apply=%region_4.5 | reduce | flops 1048576 | bytes 4194306 | tf_op jit(solution)/shard_map/reduce_sum | solution.py:189
  29.6 10.0 %scatter_custom_fusion.1 = bf16[4096,256]{1,0:T(8,128)(2,1)S(1)} fusion(s32[2048]{0:T(1024)S(1)} %bitcast.35, bf16[2048,256]{1,0:T(8,128)(2,1)S(1)} %reduce_sum.25, bf16[]{:T(256)} %constant.22.clone.1), kind=kCustom, calls=%fused_computation.5 | custom fusion | bytes 2097154 | tf_op jit(solution)/shard_map/scatter | solution.py:194
  39.6 0.0 all-to-all-done
  39.6 53.4 %all_to_all.14 = bf16[32,128,256]{2,1,0:T(8,128)(2,1)S(1)} all-to-all(bf16[32,128,256]{2,1,0:T(8,128)(2,1)S(1)} %bitcast.25), channel_id=1, replica_groups=mesh['cell'=8,'own'=4] {'cell','own'}, dimensions={0} | all-to-all | bytes 4194304 | tf_op jit(solution)/shard_map/all_to_all | solution.py:196
  93.0 0.0 copy-start
  93.0 0.0 copy-start.1
  93.0 0.0 copy-start.2
  93.0 2.7 %fusion.cell_ref = f32[1024,256]{1,0:T(8,128)S(1)} fusion(bf16[4096,256]{1,0:T(8,128)(2,1)S(1)} %bitcast.26, s32[4096]{0:T(1024)S(1)} %bitcast.33), kind=kOutput, calls=%fused_computation.3 | convolution fusion | flops 2151677952 | bytes 3162112 | tf_op jit(solution)/shard_map/dot_general | solution.py:201
  95.7 3.3 %collective-permute-start = (f32[8,256]{1,0:T(8,128)S(1)}, f32[8,256]{1,0:T(8,128)S(1)}, u32[]{:S(2)}, u32[]{:S(2)}) collective-permute-start(f32[8,256]{1,0:T(8,128)S(1)} %get-tuple-element.7), channel_id=1, source_target_pairs={{0,1},{1,2},{2,3},{3,4},{4,5},{5,6},{6,7},{7,8},{8,9},{9,10},{10,1... | collective-permute-start | bytes 24584 | tf_op jit(solution)/shard_map/ppermute | solution.py:204
  99.0 2.1 %collective-permute-start.1 = (f32[8,256]{1,0:T(8,128)S(1)}, f32[8,256]{1,0:T(8,128)S(1)}, u32[]{:S(2)}, u32[]{:S(2)}) collective-permute-start(f32[8,256]{1,0:T(8,128)S(1)} %get-tuple-element.6), channel_id=1, source_target_pairs={{1,0},{2,1},{3,2},{4,3},{5,4},{6,5},{7,6},{8,7},{9,8},{10,9},{11,1... | collective-permute-start | bytes 24584 | tf_op jit(solution)/shard_map/ppermute | solution.py:205
  101.1 0.0 collective-permute-done.low_ref
  101.1 4.6 %collective-permute-done.1.high_ref = f32[8,256]{1,0:T(8,128)S(1)} collective-permute-done((f32[8,256]{1,0:T(8,128)S(1)}, f32[8,256]{1,0:T(8,128)S(1)}, u32[]{:S(2)}, u32[]{:S(2)}) %collective-permute-start.1) | collective-permute-done | bytes 8224 | tf_op jit(solution)/shard_map/ppermute | solution.py:205
  105.8 0.0 copy-done
  105.8 0.0 copy-done.1
  105.8 0.0 copy-done.2
  105.8 9.4 %fit.1 = (f32[2,6,1024]{2,1,0:T(8,128)S(1)}, f32[2,1024]{1,0:T(2,128)}) custom-call(f32[1024,256]{1,0:T(8,128)S(1)} %fusion.cell_ref, f32[8,256]{1,0:T(8,128)S(1)} %collective-permute-done.low_ref, f32[8,256]{1,0:T(8,128)S(1)} %collective-permute-done.1.high_ref, s32[4,1024]{1,0:T(4,128)S(1)} %copy-done.1, bf16[32,256]{1,0:T(8,128)(2,1)S(1)} %copy-done.2, ...), custom_call_target="tpu_custom_call" | custom-call | tf_op jit(solution)/shard_map/fit/pallas_call | solution.py:163
  115.2 0.7 copy.11
  (2 shorter events, 0.0 us)
Async XLA Ops:
  0.6 10.6 %copy-start.3 = (s32[2048,1]{0,1:T(1,128)S(1)}, s32[2048,1]{0,1:T(1,128)}, u32[]{:S(2)}) copy-start(s32[2048,1]{0,1:T(1,128)} %param.7) | copy-start | bytes 24580
  20.2 19.4 %all-to-all-start = ((s32[32,1,128]{2,1,0:T(1,128)}), s32[32,1,128]{2,1,0:T(1,128)S(1)}, u32[]{:S(2)}, u32[]{:S(2)}) async-start(s32[32,1,128]{2,1,0:T(1,128)} %bitcast.7), calls=%async_computation | async-start | bytes 32768 | tf_op jit(solution)/shard_map/all_to_all | solution.py:197
  93.0 12.8 %copy-start = (bf16[128,32]{1,0:T(8,128)(2,1)S(1)}, bf16[128,32]{1,0:T(8,128)(2,1)}, u32[]{:S(2)}) copy-start(bf16[128,32]{1,0:T(8,128)(2,1)} %constant.24.clone.spread_ref) | copy-start | bytes 24580
  93.0 12.8 %copy-start.1 = (s32[4,1024]{1,0:T(4,128)S(1)}, s32[4,1024]{1,0:T(4,128)}, u32[]{:S(2)}) copy-start(s32[4,1024]{1,0:T(4,128)} %off_ref.1) | copy-start | bytes 49156
  93.0 12.8 %copy-start.2 = (bf16[32,256]{1,0:T(8,128)(2,1)S(1)}, bf16[32,256]{1,0:T(8,128)(2,1)}, u32[]{:S(2)}) copy-start(bf16[32,256]{1,0:T(8,128)(2,1)} %constant.23.clone.gather_ref) | copy-start | bytes 49156
  95.7 5.4 %collective-permute-start = (f32[8,256]{1,0:T(8,128)S(1)}, f32[8,256]{1,0:T(8,128)S(1)}, u32[]{:S(2)}, u32[]{:S(2)}) collective-permute-start(f32[8,256]{1,0:T(8,128)S(1)} %get-tuple-element.7), channel_id=1, source_target_pairs={{0,1},{1,2},{2,3},{3,4},{4,5},{5,6},{6,7},{7,8},{8,9},{9,10},{10,1... | collective-permute-start | bytes 24584 | tf_op jit(solution)/shard_map/ppermute | solution.py:204
  99.0 6.8 %collective-permute-start.1 = (f32[8,256]{1,0:T(8,128)S(1)}, f32[8,256]{1,0:T(8,128)S(1)}, u32[]{:S(2)}, u32[]{:S(2)}) collective-permute-start(f32[8,256]{1,0:T(8,128)S(1)} %get-tuple-element.6), channel_id=1, source_target_pairs={{1,0},{2,1},{3,2},{4,3},{5,4},{6,5},{7,6},{8,7},{9,8},{10,9},{11,1... | collective-permute-start | bytes 24584 | tf_op jit(solution)/shard_map/ppermute | solution.py:205
where the time goes:
time: 116 us
  blocking collectives  53.4 us (46%)
  local copies, waits for them, and re-layouts  19.8 us (17%)
  other arithmetic  13.3 us (11%)
  starting transfers between devices  11.8 us (10%)
  Pallas kernels  9.39 us (8%)
  waiting for transfers between devices  4.65 us (4%)
  matrix products  2.73 us (2%)
    all_to_all x1, blocking collectives, body(): lax.all_to_all(send_rows.reshape(devices, capacity, width), ('cell', 'own...  53.4 us
    scatter x1, local copies, waits for them, and re-layouts, body(): jnp.zeros((devices * capacity, width), jnp.bfloat16).at[position]  9.99 us
    pallas_call x1, Pallas kernels, fit(): pl.pallas_call(fit_kernel, out_shape=(jax.ShapeDtypeStruct((SPEC, MOM, ce...  9.39 us
    another operation x2, other arithmetic  9.27 us
    scatter x1, local copies, waits for them, and re-layouts, body(): jnp.full((devices * capacity,), -1, jnp.int32).at[position].set(cell_in)  8.79 us
    all_to_all x1, starting transfers between devices, body(): lax.all_to_all(send_cells.reshape(devices, capacity), ('cell', 'own'), sp...  6.39 us
    ppermute x1, waiting for transfers between devices, body(): high = lax.ppermute(cellhist[:RIM], ('cell', 'own'), backward)  4.65 us
    ppermute x1, starting transfers between devices, body(): low = lax.ppermute(cellhist[-RIM:], ('cell', 'own'), forward)  3.27 us
  transfers between devices with their start and end apart: 3, of which 1 were waited for; matrix products, arithmetic and copies ran while one was open for 11% of the time, Pallas kernels for 0%

commit v1 on v0

--- a/solution.py
+++ b/solution.py
@@ -146,7 +146,7 @@
         for block in range(tiles):
             cols = slice(block * TILE, (block + 1) * TILE)
             group = s * tiles + block
-            lam_ref[s, :, cols] = lam[0:MOM, group, :]
+            lam_ref[:, s, cols] = lam[0:MOM, group, :]
             value = exponent(group)
             norm = jnp.log(jnp.sum(jnp.exp(value), axis=0, keepdims=True))
             field = target[group]
@@ -163,7 +163,7 @@
     return pl.pallas_call(
         fit_kernel,
         out_shape=(
-            jax.ShapeDtypeStruct((SPEC, MOM, cells), F32),
+            jax.ShapeDtypeStruct((MOM, SPEC, cells), F32),
             jax.ShapeDtypeStruct((SPEC, cells), F32),
         ),
         in_specs=[pl.BlockSpec(memory_space=pltpu.VMEM)] * 6,
@@ -180,30 +180,213 @@
     )(cellhist, low, high, offsets, gather, spread)
 
 
+def route_kernel(n, own_n, hist_ref, dest_ref, cell_ref, out_ref, low_ref, high_ref,
+                 packed, rel, ones, send_rows, recv_rows, send_cells, recv_cells, part_out, part_in,
+                 edge_out, edge_in, row_send, row_recv, cell_send, cell_recv, part_send, part_recv,
+                 edge_send, edge_recv):
+    half = n // 2
+    rows, width = packed.shape
+    cap = ones.shape[0]
+    cells = out_ref.shape[0]
+    tiles = cells // TILE
+    me = lax.axis_index("cell") * own_n + lax.axis_index("own")
+    mine = lax.rem(me, half)
+    base = me - mine
+    cross = mine + (half - base)
+    after, before = lax.rem(me + 1, n), lax.rem(me + n - 1, n)
+
+    def place(index):
+        return (lax.div(index, own_n), lax.rem(index, own_n))
+
+    def row_copy(kind, source, slot, peer):
+        return pltpu.make_async_remote_copy(
+            src_ref=send_rows.at[kind, source], dst_ref=recv_rows.at[kind, slot],
+            send_sem=row_send.at[kind, source], recv_sem=row_recv.at[kind, slot],
+            device_id=place(base + peer), device_id_type=pl.DeviceIdType.MESH)
+
+    def cell_copy(source, slot, peer):
+        return pltpu.make_async_remote_copy(
+            src_ref=send_cells.at[source], dst_ref=recv_cells.at[slot],
+            send_sem=cell_send.at[source], recv_sem=cell_recv.at[slot],
+            device_id=place(base + peer), device_id_type=pl.DeviceIdType.MESH)
+
+    def part_copy(tile):
+        return pltpu.make_async_remote_copy(
+            src_ref=part_out.at[tile], dst_ref=part_in.at[tile],
+            send_sem=part_send.at[tile], recv_sem=part_recv.at[tile],
+            device_id=place(cross), device_id_type=pl.DeviceIdType.MESH)
+
+    def edge_copy(side):
+        return pltpu.make_async_remote_copy(
+            src_ref=edge_out.at[side], dst_ref=edge_in.at[side],
+            send_sem=edge_send.at[side], recv_sem=edge_recv.at[side],
+            device_id=place(after if side == 0 else before), device_id_type=pl.DeviceIdType.MESH)
+
+    barrier = pltpu.get_barrier_semaphore()
+
+    def greet(index):
+        pl.semaphore_signal(barrier, inc=1, device_id=place(index), device_id_type=pl.DeviceIdType.MESH)
+
+    def partners(action):
+        def one(step, carry):
+            action(lax.rem(mine + step, half))
+            return carry
+
+        lax.fori_loop(1, half, one, 0)
+
+    partners(lambda peer: greet(base + peer))
+    greet(cross)
+    greet(after)
+    greet(before)
+
+    shifted = dest_ref[...] - base
+    rel[...] = jnp.where(shifted < 0, shifted + n, shifted)
+    packed[...] = (
+        hist_ref[0].astype(F32) + hist_ref[1].astype(F32) + hist_ref[2].astype(F32)
+    ).astype(BF)
+    upto = (
+        lax.broadcasted_iota(jnp.int32, (TILE, TILE), 0) <= lax.broadcasted_iota(jnp.int32, (TILE, TILE), 1)
+    ).astype(F32).astype(BF)
+    block = lax.broadcasted_iota(jnp.int32, (n, TILE), 0)
+    slot = lax.broadcasted_iota(jnp.int32, (cap, TILE), 0).astype(F32)
+    seen = jnp.zeros((n, 1), F32)
+    slots = jnp.zeros((2 * n, cap), F32)
+    for piece in range(rows // TILE):
+        cols = slice(piece * TILE, (piece + 1) * TILE)
+        member = (block == rel[:, cols]).astype(F32)
+        count = jnp.dot(member.astype(BF), upto, preferred_element_type=F32) + seen
+        rank = jnp.sum(member * count, axis=0, keepdims=True) - 1.0
+        seen = count[:, TILE - 1 :]
+        hot = (slot == rank).astype(F32).astype(BF)
+        ones[:, cols] = hot
+        cell = cell_ref[:, cols]
+        major = (cell >> 5).astype(F32)
+        minor = (cell & 31).astype(F32)
+        named = jnp.concatenate([member * major, member * minor], axis=0).astype(BF)
+        slots = slots + lax.dot_general(named, hot, (((1,), (1,)), ((), ())), preferred_element_type=F32)
+    numbers = (32.0 * slots[:n] + slots[n:]).astype(jnp.int32)
+    send_cells[:, 0, :] = numbers[:half]
+    send_cells[:, 1, :] = numbers[half:]
+
+    def pack(kind, peer):
+        chosen = (rel[...] == kind * half + peer).astype(F32).astype(BF)
+        return jnp.dot(ones[...] * chosen, packed[...], preferred_element_type=F32).astype(BF)
+
+    pl.semaphore_wait(barrier, half + 2)
+
+    def first(peer):
+        cell_copy(peer, mine, peer).start()
+        send_rows[1, peer] = pack(1, peer)
+        row_copy(1, peer, mine, peer).start()
+
+    partners(first)
+    recv_rows[1, mine] = pack(1, mine)
+    recv_cells[mine] = send_cells[mine]
+
+    def second(peer):
+        send_rows[0, peer] = pack(0, peer)
+
+    partners(second)
+    recv_rows[0, mine] = pack(0, mine)
+
+    def arrived(kind):
+        def one(peer):
+            if kind == 1:
+                cell_copy(peer, peer, peer).wait_recv()
+            row_copy(kind, peer, peer, peer).wait_recv()
+
+        partners(one)
+        return jnp.concatenate([recv_cells[s, kind : kind + 1, :] for s in range(half)], axis=1)
+
+    def gathered(kind, names, tile):
+        cell = lax.broadcasted_iota(jnp.int32, (TILE, half * cap), 0) + tile * TILE
+        select = (cell == names).astype(F32).astype(BF)
+        return jnp.dot(select, recv_rows[kind].reshape(half * cap, width), preferred_element_type=F32)
+
+    order = [0, tiles - 1] + list(range(1, tiles - 1))
+    names = arrived(1)
+    for tile in order:
+        part_out[tile] = gathered(1, names, tile).astype(BF)
+        part_copy(tile).start()
+    partners(lambda peer: row_copy(0, peer, mine, peer).start())
+    names = arrived(0)
+    for tile in order:
+        out_ref[tile * TILE : (tile + 1) * TILE, :] = gathered(0, names, tile)
+    for at, tile in enumerate(order):
+        part_copy(tile).wait_recv()
+        span = slice(tile * TILE, (tile + 1) * TILE)
+        out_ref[span, :] = out_ref[span, :] + part_in[tile].astype(F32)
+        if at == 1:
+            edge_out[0] = out_ref[cells - RIM :, :]
+            edge_out[1] = out_ref[:RIM, :]
+            edge_copy(0).start()
+            edge_copy(1).start()
+    edge_copy(0).wait_recv()
+    edge_copy(1).wait_recv()
+    low_ref[...] = jnp.where(me == 0, 0.0, edge_in[0])
+    high_ref[...] = jnp.where(me == n - 1, 0.0, edge_in[1])
+
+    def sent(peer):
+        cell_copy(peer, mine, peer).wait_send()
+        row_copy(0, peer, mine, peer).wait_send()
+        row_copy(1, peer, mine, peer).wait_send()
+
+    partners(sent)
+    for tile in order:
+        part_copy(tile).wait_send()
+    edge_copy(0).wait_send()
+    edge_copy(1).wait_send()
+
+
+def route(hist, dest, cell_in, cells):
+    replicas, rows, width = hist.shape
+    n, own_n = lax.axis_size(("cell", "own")), lax.axis_size("own")
+    half, cap, tiles = n // 2, 2 * rows // n, cells // TILE
+    dma = pltpu.SemaphoreType.DMA
+    return pl.pallas_call(
+        functools.partial(route_kernel, n, own_n),
+        out_shape=(
+            jax.ShapeDtypeStruct((cells, width), F32),
+            jax.ShapeDtypeStruct((RIM, width), F32),
+            jax.ShapeDtypeStruct((RIM, width), F32),
+        ),
+        in_specs=[pl.BlockSpec(memory_space=pltpu.VMEM)] * 3,
+        out_specs=(pl.BlockSpec(memory_space=pltpu.VMEM),) * 3,
+        scratch_shapes=[
+            pltpu.VMEM((rows, width), BF),
+            pltpu.VMEM((1, rows), jnp.int32),
+            pltpu.VMEM((cap, rows), BF),
+            pltpu.VMEM((2, half, cap, width), BF),
+            pltpu.VMEM((2, half, cap, width), BF),
+            pltpu.VMEM((half, 2, cap), jnp.int32),
+            pltpu.VMEM((half, 2, cap), jnp.int32),
+            pltpu.VMEM((tiles, TILE, width), BF),
+            pltpu.VMEM((tiles, TILE, width), BF),
+            pltpu.VMEM((2, RIM, width), F32),
+            pltpu.VMEM((2, RIM, width), F32),
+            dma((2, half)),
+            dma((2, half)),
+            dma((half,)),
+            dma((half,)),
+            dma((tiles,)),
+            dma((tiles,)),
+            dma((2,)),
+            dma((2,)),
+        ],
+        compiler_params=pltpu.CompilerParams(
+            collective_id=0, has_side_effects=True, vmem_limit_bytes=40 * 1024 * 1024
+        ),
+        name="route",
+    )(hist, dest, cell_in)
+
+
 def body(hist, dest, cell_in, offsets):
     rows = hist.shape[0]
-    width = hist.shape[2]
-    cells = offsets.shape[1]
-    devices = lax.axis_size(("cell", "own"))
-    capacity = 2 * rows // devices
-    packed = jnp.sum(hist, axis=1, dtype=jnp.float32).astype(jnp.bfloat16)
-    target_block = dest[:, 0]
-    member = (target_block[:, None] == jnp.arange(devices, dtype=jnp.int32)[None, :]).astype(jnp.int32)
-    ranks = jnp.sum((jnp.cumsum(member, axis=0) - 1) * member, axis=1)
-    position = target_block * capacity + ranks
-    send_rows = jnp.zeros((devices * capacity, width), jnp.bfloat16).at[position].set(packed)
-    send_cells = jnp.full((devices * capacity,), -1, jnp.int32).at[position].set(cell_in)
-    got_rows = lax.all_to_all(send_rows.reshape(devices, capacity, width), ("cell", "own"), split_axis=0, concat_axis=0, tiled=True)
-    got_cells = lax.all_to_all(send_cells.reshape(devices, capacity), ("cell", "own"), split_axis=0, concat_axis=0, tiled=True)
-    recv_rows = got_rows.reshape(devices * capacity, width)
-    recv_cells = got_cells.reshape(devices * capacity)
-    select = (recv_cells[None, :] == jnp.arange(cells, dtype=jnp.int32)[:, None]).astype(jnp.bfloat16)
-    cellhist = jnp.dot(select, recv_rows, preferred_element_type=jnp.float32)
-    forward = [(i, i + 1) for i in range(devices - 1)]
-    backward = [(i + 1, i) for i in range(devices - 1)]
-    low = lax.ppermute(cellhist[-RIM:], ("cell", "own"), forward)
-    high = lax.ppermute(cellhist[:RIM], ("cell", "own"), backward)
-    return fit(cellhist, low, high, offsets)
+    cellhist, low, high = route(
+        jnp.transpose(hist, (1, 0, 2)), dest.reshape(1, rows), cell_in.reshape(1, rows), offsets.shape[1]
+    )
+    lam, stat = fit(cellhist, low, high, offsets)
+    return jnp.transpose(lam, (1, 0, 2)), stat
 
 
 def solution(mesh):

time: 116 us -> 71.1 us (0.61)
  the two profiles are of different devices: /device:TPU:7 before, /device:TPU:0 now
where the time goes in v1:
time: 71.1 us; the launch traced here: 70.9 us
  Pallas kernels  66.9 us (94%)
  local copies, waits for them, and re-layouts  3.29 us (5%)
    pallas_call x1, Pallas kernels, route(): pl.pallas_call(functools.partial(route_kernel, n, own_n), out_shape=(jax....  57.5 us
    pallas_call x1, Pallas kernels, fit(): pl.pallas_call(fit_kernel, out_shape=(jax.ShapeDtypeStruct((MOM, SPEC, ce...  9.41 us
    unnamed x12, local copies, waits for them, and re-layouts  3.29 us

profile of v1, /device:TPU:0, one launch (start us, length us, event | category | flops | bytes accessed | tf_op | source)
XLA Modules:
  0.0 70.9 jit_solution(17372222026591589729)
XLA Ops:
  0.6 0.0 copy-start
  0.6 1.9 %copy-done = bf16[2048,3,256]{2,0,1:T(8,128)(2,1)S(1)} copy-done((bf16[2048,3,256]{2,0,1:T(8,128)(2,1)S(1)}, bf16[2048,3,256]{2,0,1:T(8,128)(2,1)}, u32[]{:S(2)}) %copy-start) | copy-done | bytes 3145752
  2.5 0.0 copy-start.4
  2.5 0.7 copy-done.4
  3.2 0.0 copy-start.5
  3.2 0.7 copy-done.5
  3.9 0.0 copy-start.1
  3.9 0.0 copy-start.2
  3.9 0.0 copy-start.3
  3.9 57.5 %route.1 = (f32[1024,256]{1,0:T(8,128)S(1)}, f32[8,256]{1,0:T(8,128)S(1)}, f32[8,256]{1,0:T(8,128)S(1)}) custom-call(bf16[3,2048,256]{2,1,0:T(8,128)(2,1)S(1)} %bitcast.4, s32[1,2048]{1,0:T(1,128)S(1)} %bitcast.5, s32[1,2048]{1,0:T(1,128)S(1)} %bitcast.6), custom_call_target="tpu_custom_call" | custom-call | tf_op jit(solution)/shard_map/route/pallas_call | solution.py:346
  61.4 0.0 copy-done.1
  61.4 0.0 copy-done.2
  61.4 0.0 copy-done.3
  61.5 9.4 %fit.1 = (f32[6,2,1024]{2,1,0:T(2,128)}, f32[2,1024]{1,0:T(2,128)}) custom-call(f32[1024,256]{1,0:T(8,128)S(1)} %get-tuple-element.7.cell_ref, f32[8,256]{1,0:T(8,128)S(1)} %get-tuple-element.8.low_ref, f32[8,256]{1,0:T(8,128)S(1)} %get-tuple-element.9.high_ref, s32[4,1024]{1,0:T(4,128)S(1)} %copy-done.2, bf16[32,256]{1,0:T(8,128)(2,1)S(1)} %copy-done.3, ...), custom_call_target="tpu_custom_call" | custom-call | tf_op jit(solution)/shard_map/fit/pallas_call | solution.py:163
Async XLA Ops:
  0.6 1.9 %copy-start = (bf16[2048,3,256]{2,0,1:T(8,128)(2,1)S(1)}, bf16[2048,3,256]{2,0,1:T(8,128)(2,1)}, u32[]{:S(2)}) copy-start(bf16[2048,3,256]{2,0,1:T(8,128)(2,1)} %param.6) | copy-start | bytes 9437188
  2.5 0.7 copy-start.4
  3.2 0.7 copy-start.5
  3.9 57.5 %copy-start.1 = (bf16[128,32]{1,0:T(8,128)(2,1)S(1)}, bf16[128,32]{1,0:T(8,128)(2,1)}, u32[]{:S(2)}) copy-start(bf16[128,32]{1,0:T(8,128)(2,1)} %constant.5.clone.spread_ref) | copy-start | bytes 24580
  3.9 57.5 %copy-start.2 = (s32[4,1024]{1,0:T(4,128)S(1)}, s32[4,1024]{1,0:T(4,128)}, u32[]{:S(2)}) copy-start(s32[4,1024]{1,0:T(4,128)} %off_ref.1) | copy-start | bytes 49156
  3.9 57.5 %copy-start.3 = (bf16[32,256]{1,0:T(8,128)(2,1)S(1)}, bf16[32,256]{1,0:T(8,128)(2,1)}, u32[]{:S(2)}) copy-start(bf16[32,256]{1,0:T(8,128)(2,1)} %constant.4.clone.gather_ref) | copy-start | bytes 49156

commit v2 on v1

--- a/solution.py
+++ b/solution.py
@@ -101,8 +101,22 @@
     inverse = 1.0 / sums[0]
     for m in range(MOM):
         mu[m] = sums[m + 1] * inverse
-    lam[...] = jnp.zeros_like(lam)
     weights = product_weights(MOM)
+    flat = legendre_rows(levels, 2 * MOM + 1).mean(axis=1)
+    hess = np.array([
+        [sum(v * flat[k] for k, v in weights[max(m, n), min(m, n)]) - flat[m] * flat[n] + 0.01 * (m == n)
+         for n in range(1, MOM + 1)]
+        for m in range(1, MOM + 1)
+    ])
+    solved = 0.5 * np.linalg.inv(hess)
+    for m in range(MOM):
+        total = jnp.zeros_like(mu[0])
+        for k in range(MOM):
+            if abs(solved[m, k]) > 1e-14:
+                total = total + float(solved[m, k]) * (mu[k] - float(flat[k + 1]))
+        lam[m] = total
+    for m in range(MOM, 8):
+        lam[m] = jnp.zeros_like(mu[0])
 
     def step(_, carry):
         for group in range(SPEC * tiles):
@@ -141,7 +155,7 @@
             lam[row] = lam[row] - 0.5 * total
         return carry
 
-    lax.fori_loop(0, NEWTON, step, 0)
+    lax.fori_loop(1, NEWTON, step, 0)
     for s in range(SPEC):
         for block in range(tiles):
             cols = slice(block * TILE, (block + 1) * TILE)
@@ -180,70 +194,67 @@
     )(cellhist, low, high, offsets, gather, spread)
 
 
-def route_kernel(n, own_n, hist_ref, dest_ref, cell_ref, out_ref, low_ref, high_ref,
-                 packed, rel, ones, send_rows, recv_rows, send_cells, recv_cells, part_out, part_in,
-                 edge_out, edge_in, row_send, row_recv, cell_send, cell_recv, part_send, part_recv,
-                 edge_send, edge_recv):
+def route_kernel(n, own_n, hist_hbm, dest_hbm, cell_hbm, out_ref, low_ref, high_ref,
+                 hist, dest, cell_in, packed, rel, ones, near_out, near_in, far_out, far_in,
+                 send_cells, recv_cells, part_out, part_in, edge_out, edge_in,
+                 load, near_send, near_recv, far_send, far_recv, cell_send, cell_recv,
+                 part_send, part_recv, edge_send, edge_recv):
     half = n // 2
     rows, width = packed.shape
+    levels = width // SPEC
     cap = ones.shape[0]
     cells = out_ref.shape[0]
     tiles = cells // TILE
     me = lax.axis_index("cell") * own_n + lax.axis_index("own")
-    mine = lax.rem(me, half)
-    base = me - mine
-    cross = mine + (half - base)
     after, before = lax.rem(me + 1, n), lax.rem(me + n - 1, n)
+    bits = [lax.rem(lax.div(me, 1 << b), 2) for b in range(n.bit_length() - 1)]
+
+    def flipped(mask):
+        index = me
+        for b, bit in enumerate(bits):
+            if mask >> b & 1:
+                index = index + (1 << b) * (1 - 2 * bit)
+        return index
 
     def place(index):
         return (lax.div(index, own_n), lax.rem(index, own_n))
 
-    def row_copy(kind, source, slot, peer):
+    def remote(source, target, sent, received, index):
         return pltpu.make_async_remote_copy(
-            src_ref=send_rows.at[kind, source], dst_ref=recv_rows.at[kind, slot],
-            send_sem=row_send.at[kind, source], recv_sem=row_recv.at[kind, slot],
-            device_id=place(base + peer), device_id_type=pl.DeviceIdType.MESH)
-
-    def cell_copy(source, slot, peer):
-        return pltpu.make_async_remote_copy(
-            src_ref=send_cells.at[source], dst_ref=recv_cells.at[slot],
-            send_sem=cell_send.at[source], recv_sem=cell_recv.at[slot],
-            device_id=place(base + peer), device_id_type=pl.DeviceIdType.MESH)
-
-    def part_copy(tile):
-        return pltpu.make_async_remote_copy(
-            src_ref=part_out.at[tile], dst_ref=part_in.at[tile],
-            send_sem=part_send.at[tile], recv_sem=part_recv.at[tile],
-            device_id=place(cross), device_id_type=pl.DeviceIdType.MESH)
+            src_ref=source, dst_ref=target, send_sem=sent, recv_sem=received,
+            device_id=place(index), device_id_type=pl.DeviceIdType.MESH)
+
+    def near_copy(mask):
+        return remote(near_out.at[mask], near_in.at[mask], near_send.at[mask], near_recv.at[mask], flipped(mask))
+
+    def far_copy(s, mask):
+        return remote(far_out.at[s, mask], far_in.at[s, mask], far_send.at[s, mask], far_recv.at[s, mask], flipped(mask))
+
+    def cell_copy(mask):
+        return remote(send_cells.at[mask], recv_cells.at[mask], cell_send.at[mask], cell_recv.at[mask], flipped(mask))
+
+    def part_copy(s, tile):
+        return remote(part_out.at[s, tile], part_in.at[s, tile], part_send.at[s, tile], part_recv.at[s, tile], flipped(half))
 
     def edge_copy(side):
-        return pltpu.make_async_remote_copy(
-            src_ref=edge_out.at[side], dst_ref=edge_in.at[side],
-            send_sem=edge_send.at[side], recv_sem=edge_recv.at[side],
-            device_id=place(after if side == 0 else before), device_id_type=pl.DeviceIdType.MESH)
+        return remote(edge_out.at[side], edge_in.at[side], edge_send.at[side], edge_recv.at[side],
+                      after if side == 0 else before)
+
+    loads = [
+        pltpu.make_async_copy(dest_hbm, dest, load.at[0]),
+        pltpu.make_async_copy(cell_hbm, cell_in, load.at[1]),
+        pltpu.make_async_copy(hist_hbm, hist, load.at[2]),
+    ]
+    for copy in loads:
+        copy.start()
 
     barrier = pltpu.get_barrier_semaphore()
-
-    def greet(index):
+    for index in [flipped(mask) for mask in range(1, half + 1)] + [after, before]:
         pl.semaphore_signal(barrier, inc=1, device_id=place(index), device_id_type=pl.DeviceIdType.MESH)
 
-    def partners(action):
-        def one(step, carry):
-            action(lax.rem(mine + step, half))
-            return carry
-
-        lax.fori_loop(1, half, one, 0)
-
-    partners(lambda peer: greet(base + peer))
-    greet(cross)
-    greet(after)
-    greet(before)
-
-    shifted = dest_ref[...] - base
-    rel[...] = jnp.where(shifted < 0, shifted + n, shifted)
-    packed[...] = (
-        hist_ref[0].astype(F32) + hist_ref[1].astype(F32) + hist_ref[2].astype(F32)
-    ).astype(BF)
+    loads[0].wait()
+    rel[...] = dest[...] ^ me
+    loads[1].wait()
     upto = (
         lax.broadcasted_iota(jnp.int32, (TILE, TILE), 0) <= lax.broadcasted_iota(jnp.int32, (TILE, TILE), 1)
     ).astype(F32).astype(BF)
@@ -259,7 +270,7 @@
         seen = count[:, TILE - 1 :]
         hot = (slot == rank).astype(F32).astype(BF)
         ones[:, cols] = hot
-        cell = cell_ref[:, cols]
+        cell = cell_in[:, cols]
         major = (cell >> 5).astype(F32)
         minor = (cell & 31).astype(F32)
         named = jnp.concatenate([member * major, member * minor], axis=0).astype(BF)
@@ -267,73 +278,105 @@
     numbers = (32.0 * slots[:n] + slots[n:]).astype(jnp.int32)
     send_cells[:, 0, :] = numbers[:half]
     send_cells[:, 1, :] = numbers[half:]
-
-    def pack(kind, peer):
-        chosen = (rel[...] == kind * half + peer).astype(F32).astype(BF)
-        return jnp.dot(ones[...] * chosen, packed[...], preferred_element_type=F32).astype(BF)
+    loads[2].wait()
+    packed[...] = (hist[0].astype(F32) + hist[1].astype(F32) + hist[2].astype(F32)).astype(BF)
+
+    def pack(kind, masks):
+        chosen = [(rel[...] == kind * half + mask).astype(F32).astype(BF) for mask in masks]
+        picked = jnp.concatenate([ones[...] * row for row in chosen], axis=0)
+        return jnp.dot(picked, packed[...], preferred_element_type=F32).astype(BF)
+
+    stride = half // 4
+    groups = [[q + j * stride for j in range(4)] for q in sorted(range(stride), key=lambda q: (q % 2, -q))]
 
     pl.semaphore_wait(barrier, half + 2)
-
-    def first(peer):
-        cell_copy(peer, mine, peer).start()
-        send_rows[1, peer] = pack(1, peer)
-        row_copy(1, peer, mine, peer).start()
-
-    partners(first)
-    recv_rows[1, mine] = pack(1, mine)
-    recv_cells[mine] = send_cells[mine]
-
-    def second(peer):
-        send_rows[0, peer] = pack(0, peer)
-
-    partners(second)
-    recv_rows[0, mine] = pack(0, mine)
-
-    def arrived(kind):
-        def one(peer):
-            if kind == 1:
-                cell_copy(peer, peer, peer).wait_recv()
-            row_copy(kind, peer, peer, peer).wait_recv()
-
-        partners(one)
-        return jnp.concatenate([recv_cells[s, kind : kind + 1, :] for s in range(half)], axis=1)
-
-    def gathered(kind, names, tile):
-        cell = lax.broadcasted_iota(jnp.int32, (TILE, half * cap), 0) + tile * TILE
-        select = (cell == names).astype(F32).astype(BF)
-        return jnp.dot(select, recv_rows[kind].reshape(half * cap, width), preferred_element_type=F32)
+    for mask in range(1, half):
+        cell_copy(mask).start()
+    for masks in groups:
+        value = pack(1, masks)
+        for j, mask in enumerate(masks):
+            for s in range(SPEC):
+                piece = value[j * cap : (j + 1) * cap, s * levels : (s + 1) * levels]
+                if mask == 0:
+                    far_in[s, mask] = piece
+                else:
+                    far_out[s, mask] = piece
+            if mask != 0:
+                far_copy(0, mask).start()
+    for masks in groups:
+        for mask in masks:
+            if mask != 0:
+                far_copy(1, mask).start()
+    recv_cells[0] = send_cells[0]
+    for masks in groups:
+        value = pack(0, masks)
+        for j, mask in enumerate(masks):
+            piece = value[j * cap : (j + 1) * cap]
+            if mask == 0:
+                near_in[mask] = piece
+            else:
+                near_out[mask] = piece
+
+    for mask in range(1, half):
+        cell_copy(mask).wait_recv()
+
+    def names(kind):
+        return jnp.concatenate([recv_cells[mask, kind : kind + 1, :] for mask in range(half)], axis=1)
+
+    def gathered(name, pair, value):
+        cell = lax.broadcasted_iota(jnp.int32, (TILE, half * cap), 0)
+        select = jnp.concatenate(
+            [(cell == name - tile * TILE).astype(F32).astype(BF) for tile in pair], axis=0
+        )
+        return jnp.dot(select, value, preferred_element_type=F32)
 
     order = [0, tiles - 1] + list(range(1, tiles - 1))
-    names = arrived(1)
-    for tile in order:
-        part_out[tile] = gathered(1, names, tile).astype(BF)
-        part_copy(tile).start()
-    partners(lambda peer: row_copy(0, peer, mine, peer).start())
-    names = arrived(0)
-    for tile in order:
-        out_ref[tile * TILE : (tile + 1) * TILE, :] = gathered(0, names, tile)
-    for at, tile in enumerate(order):
-        part_copy(tile).wait_recv()
-        span = slice(tile * TILE, (tile + 1) * TILE)
-        out_ref[span, :] = out_ref[span, :] + part_in[tile].astype(F32)
-        if at == 1:
-            edge_out[0] = out_ref[cells - RIM :, :]
-            edge_out[1] = out_ref[:RIM, :]
-            edge_copy(0).start()
-            edge_copy(1).start()
+    pairs = [order[i : i + 2] for i in range(0, tiles, 2)]
+    name = names(1)
+    for s in range(SPEC):
+        for mask in range(1, half):
+            far_copy(s, mask).wait_recv()
+        for pair in pairs:
+            value = gathered(name, pair, far_in[s].reshape(half * cap, levels)).astype(BF)
+            for j, tile in enumerate(pair):
+                part_out[s, tile] = value[j * TILE : (j + 1) * TILE]
+                part_copy(s, tile).start()
+    for masks in groups:
+        for mask in masks:
+            if mask != 0:
+                near_copy(mask).start()
+    for mask in range(1, half):
+        near_copy(mask).wait_recv()
+    name = names(0)
+    for pair in pairs:
+        value = gathered(name, pair, near_in[...].reshape(half * cap, width))
+        for j, tile in enumerate(pair):
+            out_ref[tile * TILE : (tile + 1) * TILE, :] = value[j * TILE : (j + 1) * TILE]
+    for s in range(SPEC):
+        lanes = slice(s * levels, (s + 1) * levels)
+        for pair in pairs:
+            for tile in pair:
+                part_copy(s, tile).wait_recv()
+                span = slice(tile * TILE, (tile + 1) * TILE)
+                out_ref[span, lanes] = out_ref[span, lanes] + part_in[s, tile].astype(F32)
+            if s == SPEC - 1 and pair is pairs[0]:
+                edge_out[0] = out_ref[cells - RIM :, :]
+                edge_out[1] = out_ref[:RIM, :]
+                edge_copy(0).start()
+                edge_copy(1).start()
     edge_copy(0).wait_recv()
     edge_copy(1).wait_recv()
     low_ref[...] = jnp.where(me == 0, 0.0, edge_in[0])
     high_ref[...] = jnp.where(me == n - 1, 0.0, edge_in[1])
 
-    def sent(peer):
-        cell_copy(peer, mine, peer).wait_send()
-        row_copy(0, peer, mine, peer).wait_send()
-        row_copy(1, peer, mine, peer).wait_send()
-
-    partners(sent)
+    for mask in range(1, half):
+        cell_copy(mask).wait_send()
+        near_copy(mask).wait_send()
+        for s in range(SPEC):
+            far_copy(s, mask).wait_send()
     for tile in order:
-        part_copy(tile).wait_send()
+        for s in range(SPEC):
+            part_copy(s, tile).wait_send()
     edge_copy(0).wait_send()
     edge_copy(1).wait_send()
 
@@ -341,7 +384,7 @@
 def route(hist, dest, cell_in, cells):
     replicas, rows, width = hist.shape
     n, own_n = lax.axis_size(("cell", "own")), lax.axis_size("own")
-    half, cap, tiles = n // 2, 2 * rows // n, cells // TILE
+    half, cap, tiles, levels = n // 2, 2 * rows // n, cells // TILE, width // SPEC
     dma = pltpu.SemaphoreType.DMA
     return pl.pallas_call(
         functools.partial(route_kernel, n, own_n),
@@ -350,31 +393,39 @@
             jax.ShapeDtypeStruct((RIM, width), F32),
             jax.ShapeDtypeStruct((RIM, width), F32),
         ),
-        in_specs=[pl.BlockSpec(memory_space=pltpu.VMEM)] * 3,
+        in_specs=[pl.BlockSpec(memory_space=pl.ANY)] * 3,
         out_specs=(pl.BlockSpec(memory_space=pltpu.VMEM),) * 3,
         scratch_shapes=[
+            pltpu.VMEM((replicas, rows, width), BF),
+            pltpu.VMEM((1, rows), jnp.int32),
+            pltpu.VMEM((1, rows), jnp.int32),
             pltpu.VMEM((rows, width), BF),
             pltpu.VMEM((1, rows), jnp.int32),
             pltpu.VMEM((cap, rows), BF),
-            pltpu.VMEM((2, half, cap, width), BF),
-            pltpu.VMEM((2, half, cap, width), BF),
+            pltpu.VMEM((half, cap, width), BF),
+            pltpu.VMEM((half, cap, width), BF),
+            pltpu.VMEM((SPEC, half, cap, levels), BF),
+            pltpu.VMEM((SPEC, half, cap, levels), BF),
             pltpu.VMEM((half, 2, cap), jnp.int32),
             pltpu.VMEM((half, 2, cap), jnp.int32),
-            pltpu.VMEM((tiles, TILE, width), BF),
-            pltpu.VMEM((tiles, TILE, width), BF),
+            pltpu.VMEM((SPEC, tiles, TILE, levels), BF),
+            pltpu.VMEM((SPEC, tiles, TILE, levels), BF),
             pltpu.VMEM((2, RIM, width), F32),
             pltpu.VMEM((2, RIM, width), F32),
-            dma((2, half)),
-            dma((2, half)),
+            dma((3,)),
             dma((half,)),
             dma((half,)),
-            dma((tiles,)),
-            dma((tiles,)),
+            dma((SPEC, half)),
+            dma((SPEC, half)),
+            dma((half,)),
+            dma((half,)),
+            dma((SPEC, tiles)),
+            dma((SPEC, tiles)),
             dma((2,)),
             dma((2,)),
         ],
         compiler_params=pltpu.CompilerParams(
-            collective_id=0, has_side_effects=True, vmem_limit_bytes=40 * 1024 * 1024
+            collective_id=0, has_side_effects=True, vmem_limit_bytes=48 * 1024 * 1024
         ),
         name="route",
     )(hist, dest, cell_in)

time: 71.1 us -> 66.1 us (0.930)
  Pallas kernels: 66.9 us -> 61.9 us
    pallas_call x1, Pallas kernels: 57.5 us -> 53.1 us  [route(): pl.pallas_call(functools.partial(route_kernel, n, own_n), out_shape=(jax....]
where the time goes in v2:
time: 66.1 us; the launch traced here: 65.8 us
  Pallas kernels  61.9 us (94%)
  local copies, waits for them, and re-layouts  3.29 us (5%)
  between operations  0.67 us (1%)
    pallas_call x1, Pallas kernels, route(): pl.pallas_call(functools.partial(route_kernel, n, own_n), out_shape=(jax....  53.1 us
    pallas_call x1, Pallas kernels, fit(): pl.pallas_call(fit_kernel, out_shape=(jax.ShapeDtypeStruct((MOM, SPEC, ce...  8.72 us
    unnamed x12, local copies, waits for them, and re-layouts  3.29 us

profile of v2, /device:TPU:0, one launch (start us, length us, event | category | flops | bytes accessed | tf_op | source)
XLA Modules:
  0.0 65.8 jit_solution(6952868398773040908)
XLA Ops:
  0.6 0.0 copy-start
  0.6 1.9 %copy-done = bf16[2048,3,256]{2,0,1:T(8,128)(2,1)S(1)} copy-done((bf16[2048,3,256]{2,0,1:T(8,128)(2,1)S(1)}, bf16[2048,3,256]{2,0,1:T(8,128)(2,1)}, u32[]{:S(2)}) %copy-start) | copy-done | bytes 3145752
  2.5 0.0 copy-start.4
  2.5 0.7 %copy-done.4 = s32[2048,1]{0,1:T(1,128)S(1)} copy-done((s32[2048,1]{0,1:T(1,128)S(1)}, s32[2048,1]{0,1:T(1,128)}, u32[]{:S(2)}) %copy-start.4) | copy-done | bytes 8216
  3.2 0.0 copy-start.5
  3.2 0.7 %copy-done.5 = s32[2048]{0:T(1024)S(1)} copy-done((s32[2048]{0:T(1024)S(1)}, s32[2048]{0:T(1024)}, u32[]{:S(2)}) %copy-start.5) | copy-done | bytes 8216
  3.9 0.0 copy-start.1
  3.9 0.0 copy-start.2
  3.9 0.0 copy-start.3
  3.9 53.1 %route.1 = (f32[1024,256]{1,0:T(8,128)S(1)}, f32[8,256]{1,0:T(8,128)S(1)}, f32[8,256]{1,0:T(8,128)S(1)}) custom-call(bf16[3,2048,256]{2,1,0:T(8,128)(2,1)S(1)} %bitcast.4, s32[1,2048]{1,0:T(1,128)S(1)} %bitcast.5, s32[1,2048]{1,0:T(1,128)S(1)} %bitcast.6), custom_call_target="tpu_custom_call" | custom-call | tf_op jit(solution)/shard_map/route/pallas_call | solution.py:389
  57.1 0.0 copy-done.1
  57.1 0.0 copy-done.2
  57.1 0.0 copy-done.3
  57.1 8.7 %fit.1 = (f32[6,2,1024]{2,1,0:T(2,128)}, f32[2,1024]{1,0:T(2,128)}) custom-call(f32[1024,256]{1,0:T(8,128)S(1)} %get-tuple-element.7.cell_ref, f32[8,256]{1,0:T(8,128)S(1)} %get-tuple-element.8.low_ref, f32[8,256]{1,0:T(8,128)S(1)} %get-tuple-element.9.high_ref, s32[4,1024]{1,0:T(4,128)S(1)} %copy-done.2, bf16[32,256]{1,0:T(8,128)(2,1)S(1)} %copy-done.3, ...), custom_call_target="tpu_custom_call" | custom-call | tf_op jit(solution)/shard_map/fit/pallas_call | solution.py:177
Async XLA Ops:
  0.6 1.9 %copy-start = (bf16[2048,3,256]{2,0,1:T(8,128)(2,1)S(1)}, bf16[2048,3,256]{2,0,1:T(8,128)(2,1)}, u32[]{:S(2)}) copy-start(bf16[2048,3,256]{2,0,1:T(8,128)(2,1)} %param.6) | copy-start | bytes 9437188
  2.5 0.7 %copy-start.4 = (s32[2048,1]{0,1:T(1,128)S(1)}, s32[2048,1]{0,1:T(1,128)}, u32[]{:S(2)}) copy-start(s32[2048,1]{0,1:T(1,128)} %param.7) | copy-start | bytes 24580
  3.2 0.7 %copy-start.5 = (s32[2048]{0:T(1024)S(1)}, s32[2048]{0:T(1024)}, u32[]{:S(2)}) copy-start(s32[2048]{0:T(1024)} %param.8) | copy-start | bytes 24580
  3.9 53.2 %copy-start.1 = (bf16[128,32]{1,0:T(8,128)(2,1)S(1)}, bf16[128,32]{1,0:T(8,128)(2,1)}, u32[]{:S(2)}) copy-start(bf16[128,32]{1,0:T(8,128)(2,1)} %constant.5.clone.spread_ref) | copy-start | bytes 24580
  3.9 53.2 %copy-start.2 = (s32[4,1024]{1,0:T(4,128)S(1)}, s32[4,1024]{1,0:T(4,128)}, u32[]{:S(2)}) copy-start(s32[4,1024]{1,0:T(4,128)} %off_ref.1) | copy-start | bytes 49156
  3.9 53.2 %copy-start.3 = (bf16[32,256]{1,0:T(8,128)(2,1)S(1)}, bf16[32,256]{1,0:T(8,128)(2,1)}, u32[]{:S(2)}) copy-start(bf16[32,256]{1,0:T(8,128)(2,1)} %constant.4.clone.gather_ref) | copy-start | bytes 49156

commit v3 on v2

--- a/solution.py
+++ b/solution.py
@@ -73,7 +73,7 @@
         return both[:16] + both[16:]
 
     def exponent(group):
-        value = lam[:, group, :]
+        value = lam[group // tiles, :, group % tiles, :]
         high = value.astype(BF).astype(F32)
         stacked = jnp.concatenate([high, high, value - high, jnp.zeros_like(high)], axis=0)
         return jnp.dot(spread_ref[...], stacked.astype(BF), preferred_element_type=F32)
@@ -97,10 +97,7 @@
             smooth = 1.0 + (0.5 * field + 0.25 * (below + above))
             group = s * tiles + block
             target[group] = smooth
-            sums[:, group, :] = moments(smooth)
-    inverse = 1.0 / sums[0]
-    for m in range(MOM):
-        mu[m] = sums[m + 1] * inverse
+            sums[s, :, block, :] = moments(smooth)
     weights = product_weights(MOM)
     flat = legendre_rows(levels, 2 * MOM + 1).mean(axis=1)
     hess = np.array([
@@ -109,20 +106,26 @@
         for m in range(1, MOM + 1)
     ])
     solved = 0.5 * np.linalg.inv(hess)
-    for m in range(MOM):
-        total = jnp.zeros_like(mu[0])
-        for k in range(MOM):
-            if abs(solved[m, k]) > 1e-14:
-                total = total + float(solved[m, k]) * (mu[k] - float(flat[k + 1]))
-        lam[m] = total
-    for m in range(MOM, 8):
-        lam[m] = jnp.zeros_like(mu[0])
-
-    def step(_, carry):
-        for group in range(SPEC * tiles):
-            sums[:, group, :] = moments(jnp.exp(exponent(group)))
-        inverse = 1.0 / sums[0]
-        mean = [None] + [sums[k] * inverse for k in range(1, 2 * MOM + 1)]
+    for s in range(SPEC):
+        inverse = 1.0 / sums[s, 0]
+        for m in range(MOM):
+            mu[s, m] = sums[s, m + 1] * inverse
+        for m in range(MOM):
+            total = jnp.zeros_like(inverse)
+            for k in range(MOM):
+                if abs(solved[m, k]) > 1e-14:
+                    total = total + float(solved[m, k]) * (mu[s, k] - float(flat[k + 1]))
+            lam[s, m] = total
+        for m in range(MOM, 8):
+            lam[s, m] = jnp.zeros_like(inverse)
+
+    def measure(s):
+        for block in range(tiles):
+            sums[s, :, block, :] = moments(jnp.exp(exponent(s * tiles + block)))
+
+    def update(s):
+        inverse = 1.0 / sums[s, 0]
+        mean = [None] + [sums[s, k] * inverse for k in range(1, 2 * MOM + 1)]
         raw = [[None] * MOM for _ in range(MOM)]
         unit = [[None] * MOM for _ in range(MOM)]
         scale = [None] * MOM
@@ -142,7 +145,7 @@
                     unit[row][col] = total * scale[col]
         forward = []
         for row in range(MOM):
-            total = mean[row + 1] - mu[row]
+            total = mean[row + 1] - mu[s, row]
             for inner in range(row):
                 total = total - unit[row][inner] * forward[inner]
             forward.append(total)
@@ -152,7 +155,15 @@
             for inner in range(row + 1, MOM):
                 total = total - unit[inner][row] * backward[inner]
             backward[row] = total
-            lam[row] = lam[row] - 0.5 * total
+            lam[s, row] = lam[s, row] - 0.5 * total
+
+    measure(0)
+
+    def step(_, carry):
+        measure(1)
+        update(0)
+        measure(0)
+        update(1)
         return carry
 
     lax.fori_loop(1, NEWTON, step, 0)
@@ -160,7 +171,7 @@
         for block in range(tiles):
             cols = slice(block * TILE, (block + 1) * TILE)
             group = s * tiles + block
-            lam_ref[:, s, cols] = lam[0:MOM, group, :]
+            lam_ref[:, s, cols] = lam[s, 0:MOM, block, :]
             value = exponent(group)
             norm = jnp.log(jnp.sum(jnp.exp(value), axis=0, keepdims=True))
             field = target[group]
@@ -185,9 +196,9 @@
         scratch_shapes=[
             pltpu.VMEM((cells + 2 * RIM, width), F32),
             pltpu.VMEM((groups, levels, TILE), F32),
-            pltpu.VMEM((16, groups, TILE), F32),
-            pltpu.VMEM((8, groups, TILE), F32),
-            pltpu.VMEM((8, groups, TILE), F32),
+            pltpu.VMEM((SPEC, 16, groups // SPEC, TILE), F32),
+            pltpu.VMEM((SPEC, 8, groups // SPEC, TILE), F32),
+            pltpu.VMEM((SPEC, 8, groups // SPEC, TILE), F32),
         ],
         compiler_params=pltpu.CompilerParams(vmem_limit_bytes=32 * 1024 * 1024),
         name="fit",
@@ -341,10 +352,10 @@
             for j, tile in enumerate(pair):
                 part_out[s, tile] = value[j * TILE : (j + 1) * TILE]
                 part_copy(s, tile).start()
-    for masks in groups:
-        for mask in masks:
-            if mask != 0:
-                near_copy(mask).start()
+        for masks in groups[s * stride // SPEC : (s + 1) * stride // SPEC]:
+            for mask in masks:
+                if mask != 0:
+                    near_copy(mask).start()
     for mask in range(1, half):
         near_copy(mask).wait_recv()
     name = names(0)
@@ -393,7 +404,7 @@
             jax.ShapeDtypeStruct((RIM, width), F32),
             jax.ShapeDtypeStruct((RIM, width), F32),
         ),
-        in_specs=[pl.BlockSpec(memory_space=pl.ANY)] * 3,
+        in_specs=[pl.BlockSpec(memory_space=pltpu.HBM)] * 3,
         out_specs=(pl.BlockSpec(memory_space=pltpu.VMEM),) * 3,
         scratch_shapes=[
             pltpu.VMEM((replicas, rows, width), BF),

time: 66.1 us -> 62.3 us (0.943)
  Pallas kernels: 61.9 us -> 58 us
    pallas_call x1, Pallas kernels: 53.1 us -> 49.7 us  [route(): pl.pallas_call(functools.partial(route_kernel, n, own_n), out_shape=(jax....]
where the time goes in v3:
time: 62.3 us; the launch traced here: 62 us
  Pallas kernels  58 us (93%)
  local copies, waits for them, and re-layouts  3.29 us (5%)
  between operations  0.67 us (1%)
    pallas_call x1, Pallas kernels, route(): pl.pallas_call(functools.partial(route_kernel, n, own_n), out_shape=(jax....  49.7 us
    pallas_call x1, Pallas kernels, fit(): pl.pallas_call(fit_kernel, out_shape=(jax.ShapeDtypeStruct((MOM, SPEC, ce...  8.32 us
    unnamed x12, local copies, waits for them, and re-layouts  3.29 us

profile of v3, /device:TPU:0, one launch (start us, length us, event | category | flops | bytes accessed | tf_op | source)
XLA Modules:
  0.0 62.0 jit_solution(17065305562625441894)
XLA Ops:
  0.6 0.0 copy-start
  0.6 1.9 %copy-done = bf16[2048,3,256]{2,0,1:T(8,128)(2,1)S(1)} copy-done((bf16[2048,3,256]{2,0,1:T(8,128)(2,1)S(1)}, bf16[2048,3,256]{2,0,1:T(8,128)(2,1)}, u32[]{:S(2)}) %copy-start) | copy-done | bytes 3145752
  2.5 0.0 copy-start.4
  2.5 0.7 %copy-done.4 = s32[2048,1]{0,1:T(1,128)S(1)} copy-done((s32[2048,1]{0,1:T(1,128)S(1)}, s32[2048,1]{0,1:T(1,128)}, u32[]{:S(2)}) %copy-start.4) | copy-done | bytes 8216
  3.2 0.0 copy-start.5
  3.2 0.7 %copy-done.5 = s32[2048]{0:T(1024)S(1)} copy-done((s32[2048]{0:T(1024)S(1)}, s32[2048]{0:T(1024)}, u32[]{:S(2)}) %copy-start.5) | copy-done | bytes 8216
  3.9 0.0 copy-start.1
  3.9 0.0 copy-start.2
  3.9 0.0 copy-start.3
  3.9 49.7 %route.1 = (f32[1024,256]{1,0:T(8,128)S(1)}, f32[8,256]{1,0:T(8,128)S(1)}, f32[8,256]{1,0:T(8,128)S(1)}) custom-call(bf16[3,2048,256]{2,1,0:T(8,128)(2,1)S(1)} %bitcast.4, s32[1,2048]{1,0:T(1,128)S(1)} %bitcast.5, s32[1,2048]{1,0:T(1,128)S(1)} %bitcast.6), custom_call_target="tpu_custom_call" | custom-call | tf_op jit(solution)/shard_map/route/pallas_call | solution.py:400
  53.6 0.0 copy-done.1
  53.6 0.0 copy-done.2
  53.7 0.0 copy-done.3
  53.7 8.3 %fit.1 = (f32[6,2,1024]{2,1,0:T(2,128)}, f32[2,1024]{1,0:T(2,128)}) custom-call(f32[1024,256]{1,0:T(8,128)S(1)} %get-tuple-element.7.cell_ref, f32[8,256]{1,0:T(8,128)S(1)} %get-tuple-element.8.low_ref, f32[8,256]{1,0:T(8,128)S(1)} %get-tuple-element.9.high_ref, s32[4,1024]{1,0:T(4,128)S(1)} %copy-done.2, bf16[32,256]{1,0:T(8,128)(2,1)S(1)} %copy-done.3, ...), custom_call_target="tpu_custom_call" | custom-call | tf_op jit(solution)/shard_map/fit/pallas_call | solution.py:188
Async XLA Ops:
  0.6 1.9 %copy-start = (bf16[2048,3,256]{2,0,1:T(8,128)(2,1)S(1)}, bf16[2048,3,256]{2,0,1:T(8,128)(2,1)}, u32[]{:S(2)}) copy-start(bf16[2048,3,256]{2,0,1:T(8,128)(2,1)} %param.6) | copy-start | bytes 9437188
  2.5 0.7 %copy-start.4 = (s32[2048,1]{0,1:T(1,128)S(1)}, s32[2048,1]{0,1:T(1,128)}, u32[]{:S(2)}) copy-start(s32[2048,1]{0,1:T(1,128)} %param.7) | copy-start | bytes 24580
  3.2 0.7 %copy-start.5 = (s32[2048]{0:T(1024)S(1)}, s32[2048]{0:T(1024)}, u32[]{:S(2)}) copy-start(s32[2048]{0:T(1024)} %param.8) | copy-start | bytes 24580
  3.9 49.7 %copy-start.1 = (bf16[128,32]{1,0:T(8,128)(2,1)S(1)}, bf16[128,32]{1,0:T(8,128)(2,1)}, u32[]{:S(2)}) copy-start(bf16[128,32]{1,0:T(8,128)(2,1)} %constant.5.clone.spread_ref) | copy-start | bytes 24580
  3.9 49.7 %copy-start.2 = (s32[4,1024]{1,0:T(4,128)S(1)}, s32[4,1024]{1,0:T(4,128)}, u32[]{:S(2)}) copy-start(s32[4,1024]{1,0:T(4,128)} %off_ref.1) | copy-start | bytes 49156
  3.9 49.7 %copy-start.3 = (bf16[32,256]{1,0:T(8,128)(2,1)S(1)}, bf16[32,256]{1,0:T(8,128)(2,1)}, u32[]{:S(2)}) copy-start(bf16[32,256]{1,0:T(8,128)(2,1)} %constant.4.clone.gather_ref) | copy-start | bytes 49156

commit v4 on v3

--- a/solution.py
+++ b/solution.py
@@ -301,8 +301,6 @@
     groups = [[q + j * stride for j in range(4)] for q in sorted(range(stride), key=lambda q: (q % 2, -q))]
 
     pl.semaphore_wait(barrier, half + 2)
-    for mask in range(1, half):
-        cell_copy(mask).start()
     for masks in groups:
         value = pack(1, masks)
         for j, mask in enumerate(masks):
@@ -314,6 +312,9 @@
                     far_out[s, mask] = piece
             if mask != 0:
                 far_copy(0, mask).start()
+        for mask in masks:
+            if mask != 0:
+                cell_copy(mask).start()
     for masks in groups:
         for mask in masks:
             if mask != 0:
@@ -436,7 +437,7 @@
             dma((2,)),
         ],
         compiler_params=pltpu.CompilerParams(
-            collective_id=0, has_side_effects=True, vmem_limit_bytes=48 * 1024 * 1024
+            collective_id=0, has_side_effects=True, vmem_limit_bytes=63 * 1024 * 1024
         ),
         name="route",
     )(hist, dest, cell_in)

time: 62.3 us -> 62.7 us (level)
  Pallas kernels: 58 us -> 59.1 us
  local copies, waits for them, and re-layouts: 3.29 us -> 2.63 us
    pallas_call x1, Pallas kernels: 49.7 us -> 50.8 us  [route(): pl.pallas_call(functools.partial(route_kernel, n, own_n), out_shape=(jax....]
    unnamed x12, local copies, waits for them, and re-layouts: 3.29 us -> 2.63 us
where the time goes in v4:
time: 62.7 us; the launch traced here: 62.4 us
  Pallas kernels  59.1 us (94%)
  local copies, waits for them, and re-layouts  2.63 us (4%)
  between operations  0.7 us (1%)
    pallas_call x1, Pallas kernels, route(): pl.pallas_call(functools.partial(route_kernel, n, own_n), out_shape=(jax....  50.8 us
    pallas_call x1, Pallas kernels, fit(): pl.pallas_call(fit_kernel, out_shape=(jax.ShapeDtypeStruct((MOM, SPEC, ce...  8.32 us
    unnamed x12, local copies, waits for them, and re-layouts  2.63 us

profile of v4, /device:TPU:0, one launch (start us, length us, event | category | flops | bytes accessed | tf_op | source)
XLA Modules:
  0.0 62.4 jit_solution(4915647226585735437)
XLA Ops:
  0.6 0.0 copy-start.1
  0.6 0.0 copy-start.3
  0.7 0.0 copy-start.2
  0.7 50.8 %route.1 = (f32[1024,256]{1,0:T(8,128)}, f32[8,256]{1,0:T(8,128)}, f32[8,256]{1,0:T(8,128)}) custom-call(bf16[3,2048,256]{2,1,0:T(8,128)(2,1)} %bitcast.4, s32[1,2048]{1,0:T(1,128)} %bitcast.5, s32[1,2048]{1,0:T(1,128)} %bitcast.6), custom_call_target="tpu_custom_call" | custom-call | tf_op jit(solution)/shard_map/route/pallas_call | solution.py:401
  51.4 0.0 copy-done.1
  51.5 0.0 copy-done.3
  51.5 0.0 copy-done.2
  51.5 0.0 copy-start
  51.5 1.2 %copy-done = f32[1024,256]{1,0:T(8,128)S(1)} copy-done((f32[1024,256]{1,0:T(8,128)S(1)}, f32[1024,256]{1,0:T(8,128)}, u32[]{:S(2)}) %copy-start) | copy-done | bytes 1048600
  52.7 0.0 copy-start.4
  52.7 0.7 %copy-done.4 = f32[8,256]{1,0:T(8,128)S(1)} copy-done((f32[8,256]{1,0:T(8,128)S(1)}, f32[8,256]{1,0:T(8,128)}, u32[]{:S(2)}) %copy-start.4) | copy-done | bytes 8216
  53.4 0.0 copy-start.5
  53.4 0.7 %copy-done.5 = f32[8,256]{1,0:T(8,128)S(1)} copy-done((f32[8,256]{1,0:T(8,128)S(1)}, f32[8,256]{1,0:T(8,128)}, u32[]{:S(2)}) %copy-start.5) | copy-done | bytes 8216
  54.1 8.3 %fit.1 = (f32[6,2,1024]{2,1,0:T(2,128)}, f32[2,1024]{1,0:T(2,128)}) custom-call(f32[1024,256]{1,0:T(8,128)S(1)} %copy-done, f32[8,256]{1,0:T(8,128)S(1)} %copy-done.4, f32[8,256]{1,0:T(8,128)S(1)} %copy-done.5, s32[4,1024]{1,0:T(4,128)S(1)} %copy-done.2, bf16[32,256]{1,0:T(8,128)(2,1)S(1)} %copy-done.3, bf16[128,32]{1,0:T(8,128)(2,1)S(1)} %copy-done.1), custom_call_target="tpu_custom_call" | custom-call | tf_op jit(solution)/shard_map/fit/pallas_call | solution.py:188
Async XLA Ops:
  0.6 50.8 %copy-start.1 = (bf16[128,32]{1,0:T(8,128)(2,1)S(1)}, bf16[128,32]{1,0:T(8,128)(2,1)}, u32[]{:S(2)}) copy-start(bf16[128,32]{1,0:T(8,128)(2,1)} %constant.5.clone.spread_ref) | copy-start | bytes 24580
  0.6 50.8 %copy-start.3 = (bf16[32,256]{1,0:T(8,128)(2,1)S(1)}, bf16[32,256]{1,0:T(8,128)(2,1)}, u32[]{:S(2)}) copy-start(bf16[32,256]{1,0:T(8,128)(2,1)} %constant.4.clone.gather_ref) | copy-start | bytes 49156
  0.7 50.8 %copy-start.2 = (s32[4,1024]{1,0:T(4,128)S(1)}, s32[4,1024]{1,0:T(4,128)}, u32[]{:S(2)}) copy-start(s32[4,1024]{1,0:T(4,128)} %off_ref.1) | copy-start | bytes 49156
  51.5 1.2 %copy-start = (f32[1024,256]{1,0:T(8,128)S(1)}, f32[1024,256]{1,0:T(8,128)}, u32[]{:S(2)}) copy-start(f32[1024,256]{1,0:T(8,128)} %get-tuple-element.7.cell_ref) | copy-start | bytes 3145732
  52.7 0.7 %copy-start.4 = (f32[8,256]{1,0:T(8,128)S(1)}, f32[8,256]{1,0:T(8,128)}, u32[]{:S(2)}) copy-start(f32[8,256]{1,0:T(8,128)} %get-tuple-element.8.low_ref) | copy-start | bytes 24580
  53.4 0.7 %copy-start.5 = (f32[8,256]{1,0:T(8,128)S(1)}, f32[8,256]{1,0:T(8,128)}, u32[]{:S(2)}) copy-start(f32[8,256]{1,0:T(8,128)} %get-tuple-element.9.high_ref) | copy-start | bytes 24580

commit v5 on v4

--- a/solution.py
+++ b/solution.py
@@ -437,7 +437,7 @@
             dma((2,)),
         ],
         compiler_params=pltpu.CompilerParams(
-            collective_id=0, has_side_effects=True, vmem_limit_bytes=63 * 1024 * 1024
+            collective_id=0, has_side_effects=True, vmem_limit_bytes=61 * 1024 * 1024 + 512 * 1024
         ),
         name="route",
     )(hist, dest, cell_in)

time: 62.7 us -> 62.7 us (level)
  no operation moved by 1% of the time
where the time goes in v5:
time: 62.7 us; the launch traced here: 62.4 us
  Pallas kernels  59.1 us (94%)
  local copies, waits for them, and re-layouts  2.63 us (4%)
  between operations  0.7 us (1%)
    pallas_call x1, Pallas kernels, route(): pl.pallas_call(functools.partial(route_kernel, n, own_n), out_shape=(jax....  50.8 us
    pallas_call x1, Pallas kernels, fit(): pl.pallas_call(fit_kernel, out_shape=(jax.ShapeDtypeStruct((MOM, SPEC, ce...  8.32 us
    unnamed x12, local copies, waits for them, and re-layouts  2.63 us

profile of v5, /device:TPU:0, one launch (start us, length us, event | category | flops | bytes accessed | tf_op | source)
XLA Modules:
  0.0 62.4 jit_solution(15996361144618861527)
XLA Ops:
  0.6 0.0 copy-start.1
  0.6 0.0 copy-start.3
  0.7 0.0 copy-start.2
  0.7 50.8 %route.1 = (f32[1024,256]{1,0:T(8,128)}, f32[8,256]{1,0:T(8,128)}, f32[8,256]{1,0:T(8,128)}) custom-call(bf16[3,2048,256]{2,1,0:T(8,128)(2,1)} %bitcast.4, s32[1,2048]{1,0:T(1,128)} %bitcast.5, s32[1,2048]{1,0:T(1,128)} %bitcast.6), custom_call_target="tpu_custom_call" | custom-call | tf_op jit(solution)/shard_map/route/pallas_call | solution.py:401
  51.4 0.0 copy-done.1
  51.5 0.0 copy-done.3
  51.5 0.0 copy-done.2
  51.5 0.0 copy-start
  51.5 1.2 %copy-done = f32[1024,256]{1,0:T(8,128)S(1)} copy-done((f32[1024,256]{1,0:T(8,128)S(1)}, f32[1024,256]{1,0:T(8,128)}, u32[]{:S(2)}) %copy-start) | copy-done | bytes 1048600
  52.7 0.0 copy-start.4
  52.7 0.7 %copy-done.4 = f32[8,256]{1,0:T(8,128)S(1)} copy-done((f32[8,256]{1,0:T(8,128)S(1)}, f32[8,256]{1,0:T(8,128)}, u32[]{:S(2)}) %copy-start.4) | copy-done | bytes 8216
  53.4 0.0 copy-start.5
  53.4 0.7 %copy-done.5 = f32[8,256]{1,0:T(8,128)S(1)} copy-done((f32[8,256]{1,0:T(8,128)S(1)}, f32[8,256]{1,0:T(8,128)}, u32[]{:S(2)}) %copy-start.5) | copy-done | bytes 8216
  54.1 8.3 %fit.1 = (f32[6,2,1024]{2,1,0:T(2,128)}, f32[2,1024]{1,0:T(2,128)}) custom-call(f32[1024,256]{1,0:T(8,128)S(1)} %copy-done, f32[8,256]{1,0:T(8,128)S(1)} %copy-done.4, f32[8,256]{1,0:T(8,128)S(1)} %copy-done.5, s32[4,1024]{1,0:T(4,128)S(1)} %copy-done.2, bf16[32,256]{1,0:T(8,128)(2,1)S(1)} %copy-done.3, bf16[128,32]{1,0:T(8,128)(2,1)S(1)} %copy-done.1), custom_call_target="tpu_custom_call" | custom-call | tf_op jit(solution)/shard_map/fit/pallas_call | solution.py:188
Async XLA Ops:
  0.6 50.8 %copy-start.1 = (bf16[128,32]{1,0:T(8,128)(2,1)S(1)}, bf16[128,32]{1,0:T(8,128)(2,1)}, u32[]{:S(2)}) copy-start(bf16[128,32]{1,0:T(8,128)(2,1)} %constant.5.clone.spread_ref) | copy-start | bytes 24580
  0.6 50.8 %copy-start.3 = (bf16[32,256]{1,0:T(8,128)(2,1)S(1)}, bf16[32,256]{1,0:T(8,128)(2,1)}, u32[]{:S(2)}) copy-start(bf16[32,256]{1,0:T(8,128)(2,1)} %constant.4.clone.gather_ref) | copy-start | bytes 49156
  0.7 50.8 %copy-start.2 = (s32[4,1024]{1,0:T(4,128)S(1)}, s32[4,1024]{1,0:T(4,128)}, u32[]{:S(2)}) copy-start(s32[4,1024]{1,0:T(4,128)} %off_ref.1) | copy-start | bytes 49156
  51.5 1.2 %copy-start = (f32[1024,256]{1,0:T(8,128)S(1)}, f32[1024,256]{1,0:T(8,128)}, u32[]{:S(2)}) copy-start(f32[1024,256]{1,0:T(8,128)} %get-tuple-element.7.cell_ref) | copy-start | bytes 3145732
  52.7 0.7 %copy-start.4 = (f32[8,256]{1,0:T(8,128)S(1)}, f32[8,256]{1,0:T(8,128)}, u32[]{:S(2)}) copy-start(f32[8,256]{1,0:T(8,128)} %get-tuple-element.8.low_ref) | copy-start | bytes 24580
  53.4 0.7 %copy-start.5 = (f32[8,256]{1,0:T(8,128)S(1)}, f32[8,256]{1,0:T(8,128)}, u32[]{:S(2)}) copy-start(f32[8,256]{1,0:T(8,128)} %get-tuple-element.9.high_ref) | copy-start | bytes 24580
